TPU v7x, 32 devices: a whole 2x2x4 slice. The times are simulated.
32 devices in a mesh: groups: 2 (over x), tp: 16 (over z, y, core).
Axes of the slice: x: 2, y: 2, z: 4, core: 2. Of those that a mesh axis runs over, the one named last changes fastest.
Arguments:
- residual: float32 [128, 16384], P(('groups', 'tp')), parts along dimension 0, may hold values from -36 to 36
- norm_gain: float32 [16384], replicated, may hold values from 0.1 to 1.9
- segment_ids: int32 [128], P('groups'), parts along dimension 0, may hold values from 0 to 3, never falling along the last dimension, each value on 1 to 32 neighbouring positions
- w_query: bfloat16 [16384, 8192], P(None, 'tp'), may hold values from -1.734375 to 1.734375
- w_key: bfloat16 [16384, 1024], P(None, 'tp'), may hold values from -0.046875 to 0.046875
- w_value: bfloat16 [16384, 1024], P(None, 'tp'), may hold values from -0.046875 to 0.046875
- w_out: bfloat16 [8192, 16384], P('tp'), may hold values from -0.1875 to 0.1875
Outputs:
- updated: float32 [128, 16384], P(('groups', 'tp')), parts along dimension 0
There are 2 independent parts, one for each index of `groups`. A program takes and returns all parts, laid end to end along the dimension named above; an argument that names none is the same for every part. Nothing has to cross between parts.
All inputs are finite; a program needn't handle non-finite values.
Results may differ from a plain program's by a relative error of at most 0.014.
Values may be sent and summed in bfloat16 or wider, within the bound.
A program may use at most 128 MiB of HBM per device.

v0:
```python
import math

import jax
import jax.numpy as jnp
from jax import lax
from jax.sharding import PartitionSpec as P

QH = 64
KVH = 8
HD = 128
BLOCK = 128


code_limit = 448.0
rope_base = 500000.0


def quantize(values):
    row_count = values.shape[0]
    blocks = values.reshape(row_count, -1, BLOCK)
    scales = ((jnp.max(jnp.abs(blocks), axis=2) + 1e-06) / code_limit).astype(jnp.bfloat16)
    encoded = (blocks / scales.astype(jnp.float32)[:, :, None]).astype(jnp.bfloat16)
    return (encoded.reshape(row_count, -1), scales)


def expand(encoded, scales):
    row_count = encoded.shape[0]
    blocks = (
        encoded.astype(jnp.float32).reshape(row_count, -1, BLOCK)
        * scales.astype(jnp.float32)[:, :, None]
    )
    return blocks.reshape(row_count, -1)


def positions_of(segment_ids):
    token_count = segment_ids.shape[0]
    token_index = jnp.arange(token_count, dtype=jnp.int32)
    change = jnp.concatenate([jnp.ones((1,), dtype=bool), segment_ids[1:] != segment_ids[:-1]])
    offset = lax.cummax(jnp.where(change, token_index, jnp.zeros_like(token_index)), axis=0)
    return token_index - offset


def rotate(values, positions):
    half_dim = values.shape[-1] // 2
    inv_freq = rope_base ** (-(jnp.arange(half_dim, dtype=jnp.float32) * 2.0) / (2 * half_dim))
    angles = positions.astype(jnp.float32)[:, None] * inv_freq[None, :]
    cosine = jnp.cos(angles)[:, None, :]
    sine_vals = jnp.sin(angles)[:, None, :]
    first_half = values[..., :half_dim].astype(jnp.float32)
    second = values[..., half_dim:].astype(jnp.float32)
    return jnp.concatenate(
        [first_half * cosine - second * sine_vals, second * cosine + first_half * sine_vals],
        axis=-1,
    )


def attend(queries, chosen_keys, chosen_values, segment_ids):
    token_count = queries.shape[0]
    token_index = jnp.arange(token_count, dtype=jnp.int32)
    scores = jnp.einsum(
        "qhd,khd->hqk", queries, chosen_keys, preferred_element_type=jnp.float32
    ) / math.sqrt(queries.shape[2])
    allowed = (token_index[None, :] <= token_index[:, None]) & (
        segment_ids[:, None] == segment_ids[None, :]
    )
    scores = jnp.where(allowed[None], scores, -1e30)
    row_max = jnp.max(scores, axis=2, keepdims=True)
    weights = jnp.exp(scores - row_max)
    probabilities = (weights / jnp.sum(weights, axis=2, keepdims=True)).astype(jnp.bfloat16)
    outputs = jnp.einsum(
        "hqk,khd->qhd", probabilities, chosen_values, preferred_element_type=jnp.float32
    )
    return outputs.astype(jnp.bfloat16).reshape(token_count, -1)


def per_device(residual, norm_gain, segment_ids, w_query, w_key, w_value, w_out):
    own_rows = residual.shape[0]
    mean_square = jnp.mean(residual * residual, axis=1, keepdims=True)
    normed = residual * lax.rsqrt(mean_square + 1e-05) * norm_gain[None, :]
    encoded, scales = quantize(normed)
    token_count = segment_ids.shape[0]
    head_cols = w_query.shape[1]
    inputs = expand(
        lax.all_gather(encoded, "tp", axis=0, tiled=True),
        lax.all_gather(scales, "tp", axis=0, tiled=True),
    ).astype(jnp.bfloat16)
    query_part = jnp.dot(inputs, w_query, preferred_element_type=jnp.float32).astype(jnp.bfloat16)
    key_part = jnp.dot(inputs, w_key, preferred_element_type=jnp.float32).astype(jnp.bfloat16)
    value_part = jnp.dot(inputs, w_value, preferred_element_type=jnp.float32).astype(jnp.bfloat16)
    key_lin, value_lin = (
        lax.all_gather(key_part, "tp", axis=1, tiled=True),
        lax.all_gather(value_part, "tp", axis=1, tiled=True),
    )
    positions = positions_of(segment_ids)
    local_heads = head_cols // HD
    queries = rotate(query_part.reshape(token_count, local_heads, HD), positions).astype(
        jnp.bfloat16
    )
    key_heads = key_lin.reshape(token_count, HD, KVH).transpose(0, 2, 1)
    rotated_keys = rotate(key_heads, positions).astype(jnp.bfloat16)
    values = value_lin.reshape(token_count, HD, KVH).transpose(0, 2, 1)
    head_ids = (lax.axis_index("tp") * local_heads + jnp.arange(local_heads, dtype=jnp.int32)) // (
        QH // KVH
    )
    chosen_keys = jnp.take(rotated_keys, head_ids, axis=1)
    chosen_values = jnp.take(values, head_ids, axis=1)
    attended = attend(queries, chosen_keys, chosen_values, segment_ids)
    partial_value = jnp.dot(attended, w_out, preferred_element_type=jnp.float32)
    part_codes, part_scales = quantize(partial_value)
    got_codes, got_scales = (
        lax.all_to_all(part_codes, "tp", split_axis=0, concat_axis=0, tiled=True),
        lax.all_to_all(part_scales, "tp", split_axis=0, concat_axis=0, tiled=True),
    )
    sources = lax.axis_size("tp")
    owner_terms = expand(got_codes, got_scales).reshape(sources, own_rows, -1)
    summed = jnp.sum(owner_terms, axis=0)
    return residual + summed


def solution(mesh):
    in_specs = (
        P(("groups", "tp"), None),
        P(),
        P("groups"),
        P(None, "tp"),
        P(None, "tp"),
        P(None, "tp"),
        P("tp", None),
    )
    out_specs = P(("groups", "tp"), None)
    return jax.shard_map(
        per_device, mesh=mesh, in_specs=in_specs, out_specs=out_specs, check_vma=False
    )
```

profile of v0, /device:TPU:15, one launch (start us, length us, event | category | flops | bytes accessed | tf_op | source)
XLA Modules:
  0.0 213.1 jit_solution(2423854892447505430)
XLA Ops:
  6.5 1.3 multiply_reduce_fusion.1
  7.9 1.1 abs_bitcast_fusion
  9.3 1.9 fusion.15
  11.2 0.8 compare_bitcast_fusion
  12.2 22.5 %copy.52 = bf16[16384,512]{1,0:T(8,128)(2,1)} copy(bf16[16384,512]{0,1:T(8,128)(2,1)} %bitcast.56) | data formatting | bytes 33554432 | tf_op jit(solution)/shard_map/dot_general | solution.py:108
  34.9 15.7 %all-gather.1 = bf16[16,4,128]{2,1,0:T(4,128)(2,1)S(1)} all-gather(bf16[1,4,128]{2,1,0:T(4,128)(2,1)S(1)} %get-tuple-element.12), channel_id=1, replica_groups=mesh['groups'=2,'tp'=16] {'tp'}, dimensions={0}, use_global_device_ids=true | all-gather | bytes 17408 | tf_op jit(solution)/shard_map/all_gather | solution.py:85
  51.0 1.5 all-gather.4.cloned.1.call-done
  52.5 4.2 %reshape.247 = f32[64,16384]{1,0:T(8,128)} reshape(bf16[16,4,16384]{2,1,0:T(4,128)(2,1)} %all-gather.4.cloned.1.call-done) | data formatting | bytes 6291456 | tf_op jit(solution)/shard_map/convert_element_type | solution.py:29
  56.7 1.1 mul.140
  57.9 1.0 copy-done.4
  58.9 2.6 %fusion.1 = bf16[64,16384]{1,0:T(8,128)(2,1)S(1)} fusion(f32[64,16384]{1,0:T(8,128)S(1)} %copy-done.4, f32[8,8,128,128]{3,2,1,0:T(8,128)S(1)} %bitcast.57), kind=kLoop, calls=%fused_computation.4 | loop fusion | flops 2097152 | bytes 10485760 | tf_op jit(solution)/shard_map/convert_element_type | solution.py:86
  61.6 1.3 copy-done.2
  62.9 0.7 convolution_convert_fusion.2
  63.7 9.5 %convolution_convert_fusion = bf16[64,512]{1,0:T(8,128)(2,1)S(1)} fusion(bf16[64,16384]{1,0:T(8,128)(2,1)} %copy-done.2, bf16[16384,512]{1,0:T(8,128)(2,1)} %param.12), kind=kOutput, calls=%fused_computation.12 | convolution fusion | flops 1073774592 | bytes 18939904 | tf_op jit(solution)/shard_map/dot_general | solution.py:87
  73.4 20.5 %all_gather.15 = bf16[64,1024]{0,1:T(8,128)(2,1)S(1)} all-gather(bf16[64,64]{0,1:T(8,128)(2,1)S(1)} %copy.43), channel_id=1, replica_groups=mesh['groups'=2,'tp'=16] {'tp'}, dimensions={1}, use_global_device_ids=true | all-gather | bytes 139264 | tf_op jit(solution)/shard_map/all_gather | solution.py:91
  94.4 0.6 gather_fusion.1
  95.5 2.3 %convolution_convert_fusion.3 = bf16[64,64]{1,0:T(8,128)(2,1)S(1)} fusion(bf16[64,16384]{1,0:T(8,128)(2,1)S(1)} %copy-done.3, bf16[16384,64]{0,1:T(8,128)(2,1)} %param.14), kind=kOutput, calls=%fused_computation.16 | convolution fusion | flops 134221824 | bytes 4202496 | tf_op jit(solution)/shard_map/dot_general | solution.py:89
  97.9 18.3 %all_gather.14 = bf16[64,1024]{0,1:T(8,128)(2,1)S(1)} all-gather(bf16[64,64]{0,1:T(8,128)(2,1)S(1)} %copy.38), channel_id=1, replica_groups=mesh['groups'=2,'tp'=16] {'tp'}, dimensions={1}, use_global_device_ids=true | all-gather | bytes 139264 | tf_op jit(solution)/shard_map/all_gather | solution.py:92
  116.4 0.6 gather_fusion
  117.3 11.7 %abs_reduce_fusion = (f32[64,128]{0,1:T(8,128)S(1)}, f32[64,128,128]{2,0,1:T(8,128)}) fusion(bf16[64,512,1]{1,0,2:T(8,128)(2,1)S(1)} %reshape.253, bf16[128,128,512]{2,1,0:T(8,128)(2,1)} %bitcast.55), kind=kOutput, calls=%fused_computation.7 | convolution fusion | flops 1075830784 | bytes 21069824 | tf_op jit(solution)/shard_map/dot_general | solution.py:108
  129.1 0.6 multiply_convert_fusion
  129.8 0.8 copy.49
  130.6 7.5 %all-to-all-start.1 = ((bf16[16,4,128]{2,1,0:T(4,128)(2,1)}), bf16[16,4,128]{2,1,0:T(4,128)(2,1)S(1)}, u32[]{:S(2)}, u32[]{:S(2)}) async-start(bf16[16,4,128]{2,1,0:T(4,128)(2,1)} %bitcast.13), calls=%async_computation.1 | async-start | bytes 32768 | tf_op jit(solution)/shard_map/all_to_all | solution.py:112
  138.1 2.9 %divide_convert_fusion = bf16[64,128,128]{2,0,1:T(8,128)(2,1)S(1)} fusion(f32[64,128,128]{2,0,1:T(8,128)} %get-tuple-element.17, f32[64,128]{0,1:T(8,128)S(1)} %copy.49), kind=kLoop, calls=%fused_computation.6 | loop fusion | flops 2097152 | bytes 6324224 | tf_op jit(solution)/shard_map/convert_element_type | solution.py:22
  141.0 2.7 %copy.50 = bf16[64,128,128]{2,1,0:T(8,128)(2,1)} copy(bf16[64,128,128]{2,0,1:T(8,128)(2,1)S(1)} %divide_convert_fusion) | data formatting | bytes 4194304 | tf_op jit(solution)/shard_map/convert_element_type | solution.py:22
  143.7 4.1 %all_to_all.10 = bf16[16,4,16384]{2,1,0:T(4,128)(2,1)} reshape(bf16[64,128,128]{2,1,0:T(8,128)(2,1)} %copy.50) | data formatting | bytes 4194304 | tf_op jit(solution)/shard_map/all_to_all | solution.py:111
  147.8 6.1 %all-to-all-start = ((bf16[16,4,16384]{2,1,0:T(4,128)(2,1)}), bf16[16,4,16384]{2,1,0:T(4,128)(2,1)}, u32[]{:S(2)}, u32[]{:S(2)}) async-start(bf16[16,4,16384]{2,1,0:T(4,128)(2,1)} %all_to_all.10), calls=%async_computation | async-start | bytes 4194304 | tf_op jit(solution)/shard_map/all_to_all | solution.py:111
  153.8 2.6 %mul.160 = f32[64,128,128]{2,1,0:T(8,128)} broadcast(bf16[64,128]{1,0:T(8,128)(2,1)S(1)} %bitcast.62), dimensions={0,1} | broadcast | bytes 4210688 | tf_op jit(solution)/shard_map/mul | solution.py:29
  156.4 5.7 %mul.161 = f32[16,4,16384]{2,1,0:T(4,128)} reshape(f32[64,128,128]{2,1,0:T(8,128)} %mul.160) | data formatting | bytes 8388608 | tf_op jit(solution)/shard_map/mul | solution.py:29
  162.1 39.2 %all-to-all-done = bf16[16,4,16384]{2,1,0:T(4,128)(2,1)} async-done(((bf16[16,4,16384]{2,1,0:T(4,128)(2,1)}), bf16[16,4,16384]{2,1,0:T(4,128)(2,1)}, u32[]{:S(2)}, u32[]{:S(2)}) %all-to-all-start) | async-done | bytes 2097184 | tf_op jit(solution)/shard_map/all_to_all | solution.py:111
  201.3 4.1 %multiply_reduce_fusion = f32[4,16384]{1,0:T(4,128)S(1)} fusion(f32[16,4,16384]{2,1,0:T(4,128)} %mul.161, bf16[16,4,16384]{2,1,0:T(4,128)(2,1)} %all-to-all-done), kind=kLoop, calls=%fused_computation.5 | loop fusion | flops 3080192 | bytes 6553600 | tf_op jit(solution)/shard_map/reduce_sum | solution.py:116
  205.5 0.8 add.58
  (45 shorter events, 2.9 us)
Async XLA Ops:
  6.5 56.4 %copy-start = (bf16[16384,64]{0,1:T(8,128)(2,1)S(1)}, bf16[16384,64]{0,1:T(8,128)(2,1)}, u32[]{:S(2)}) copy-start(bf16[16384,64]{0,1:T(8,128)(2,1)} %param.13) | copy-start | bytes 6291460
  6.5 46.0 %all-gather.4.cloned.1.call-start = ((), (), s32[]{:S(2)}) async-start(), calls=%async_computation.2 | async-start | bytes 2228224 | tf_op jit(solution)/shard_map/all_gather | solution.py:84
  12.2 38.5 %copy-start.6 = (s32[64]{0:T(128)S(1)}, s32[64]{0:T(128)}, u32[]{:S(2)}) copy-start(s32[64]{0:T(128)} %param.11) | copy-start | bytes 772
  56.7 2.2 %copy-start.4 = (f32[64,16384]{1,0:T(8,128)S(1)}, f32[64,16384]{1,0:T(8,128)}, u32[]{:S(2)}) copy-start(f32[64,16384]{1,0:T(8,128)} %reshape.247) | copy-start | bytes 12582916
  61.6 1.4 copy-start.2
  63.7 31.8 %copy-start.3 = (bf16[64,16384]{1,0:T(8,128)(2,1)S(1)}, bf16[64,16384]{1,0:T(8,128)(2,1)}, u32[]{:S(2)}) copy-start(bf16[64,16384]{1,0:T(8,128)(2,1)} %copy-done.2) | copy-start | bytes 6291460
  130.6 17.2 %all-to-all-start.1 = ((bf16[16,4,128]{2,1,0:T(4,128)(2,1)}), bf16[16,4,128]{2,1,0:T(4,128)(2,1)S(1)}, u32[]{:S(2)}, u32[]{:S(2)}) async-start(bf16[16,4,128]{2,1,0:T(4,128)(2,1)} %bitcast.13), calls=%async_computation.1 | async-start | bytes 32768 | tf_op jit(solution)/shard_map/all_to_all | solution.py:112
  147.8 53.6 %all-to-all-start = ((bf16[16,4,16384]{2,1,0:T(4,128)(2,1)}), bf16[16,4,16384]{2,1,0:T(4,128)(2,1)}, u32[]{:S(2)}, u32[]{:S(2)}) async-start(bf16[16,4,16384]{2,1,0:T(4,128)(2,1)} %all_to_all.10), calls=%async_computation | async-start | bytes 4194304 | tf_op jit(solution)/shard_map/all_to_all | solution.py:111
  156.4 49.8 %copy-start.1 = (bf16[16384,64]{0,1:T(8,128)(2,1)S(1)}, bf16[16384,64]{0,1:T(8,128)(2,1)}, u32[]{:S(2)}) copy-start(bf16[16384,64]{0,1:T(8,128)(2,1)} %param.13) | copy-start | bytes 6291460
  162.1 43.3 %copy-start.5 = (f32[4,16384]{1,0:T(4,128)S(1)}, f32[4,16384]{1,0:T(4,128)}, u32[]{:S(2)}) copy-start(f32[4,16384]{1,0:T(4,128)} %param.9) | copy-start | bytes 786436
Sparse Core Ops, SparseCore 0:
  11.4 41.1 all-gather.3
where the time goes:
time: 214 us; the launch traced here: 213 us
  blocking collectives  54.5 us (25%)
  local copies, waits for them, and re-layouts  48.4 us (23%)
  waiting for transfers between devices  40.7 us (19%)
  matrix products  25 us (12%)
  other arithmetic  17.2 us (8%)
  starting transfers between devices  13.6 us (6%)
  between operations  13.6 us (6%)
    all_to_all x1, waiting for transfers between devices, per_device(): lax.all_to_all(part_codes, 'tp', split_axis=0, concat_axis=0, tiled=True)  39.2 us
    dot_general x1, local copies, waits for them, and re-layouts, per_device(): partial_value = jnp.dot(attended, w_out, preferred_element_type=jnp.float32)  22.5 us
    all_gather x1, blocking collectives, per_device(): lax.all_gather(key_part, 'tp', axis=1, tiled=True)  20.5 us
    all_gather x1, blocking collectives, per_device(): lax.all_gather(value_part, 'tp', axis=1, tiled=True)  18.3 us
    all_gather x1, blocking collectives, per_device(): lax.all_gather(scales, 'tp', axis=0, tiled=True)  15.7 us
    dot_general x1, matrix products, per_device(): partial_value = jnp.dot(attended, w_out, preferred_element_type=jnp.float32)  11.7 us
    dot_general x1, matrix products, per_device(): jnp.dot(inputs, w_query, preferred_element_type=jnp.float32)  9.55 us
    mul x3, local copies, waits for them, and re-layouts, expand(): encoded.astype(jnp.float32).reshape(row_count, -1, BLOCK)  9.46 us
  transfers between devices with their start and end apart: 3, of which 2 were waited for; matrix products, arithmetic and copies ran while one was open for 18% of the time, Pallas kernels for 0%

commit v1 on v0

--- a/solution.py
+++ b/solution.py
@@ -1,8 +1,11 @@
+import functools
 import math
 
 import jax
 import jax.numpy as jnp
 from jax import lax
+from jax.experimental import pallas as pl
+from jax.experimental.pallas import tpu as pltpu
 from jax.sharding import PartitionSpec as P
 
 QH = 64
@@ -13,6 +16,383 @@
 
 code_limit = 448.0
 rope_base = 500000.0
+
+NZ, NY, NC = 4, 2, 2
+N = NZ * NY * NC
+OWN = 4
+SUB = 16 // OWN
+KC = 4
+RC = 8
+
+
+def one_hot(condition):
+    return jnp.where(condition, 1.0, 0.0).astype(jnp.bfloat16)
+
+
+def token_of_row(row):
+    core, y, z, tok = row // 32, (row // 16) % 2, (row // 4) % 4, row % 4
+    return ((z * NY + y) * NC + core) * OWN + tok
+
+
+def dot(a, b):
+    return jnp.dot(a, b, preferred_element_type=jnp.float32)
+
+
+def dot_t(a, b):
+    return lax.dot_general(a, b, (((1,), (1,)), ((), ())), preferred_element_type=jnp.float32)
+
+
+def layer_kernel(
+    residual, gain, segments, w_query, w_key, w_value, w_out, out,
+    pack, gathered, wq, wkv, wo, q_acc, kv_acc, kv_out, kv_in, attended,
+    core_own, core_out, core_in, y_own, y_out, y_in, z_out, z_in, total,
+    w_sem, wo_sem, g_recv, g_zsend, g_ysend, g_csend, kv_send, kv_recv,
+    c_send, c_recv, y_send, y_recv, z_send, z_recv,
+):
+    depth = w_query.shape[0]
+    chunk = depth // KC
+    width = chunk // SUB
+    cols = w_out.shape[1] // RC
+    quarter = cols // SUB
+    tokens = N * OWN
+    heads = w_query.shape[1] // HD
+    kv_cols = w_key.shape[0]
+
+    me = lax.axis_index("tp")
+    z, y, core = me // 4, (me // 2) % 2, me % 2
+    y_peer = (z * NY + (1 - y)) * NC + core
+    core_peer = (z * NY + y) * NC + (1 - core)
+
+    def at_z(zz):
+        return (zz * NY + y) * NC + core
+
+    def weight_copies(k):
+        rows = pl.ds(pl.multiple_of(k * chunk, chunk), chunk)
+        return [
+            pltpu.make_async_copy(w_query.at[rows], wq.at[rows], w_sem.at[0, k]),
+            pltpu.make_async_copy(w_key.at[:, rows], wkv.at[k, :kv_cols], w_sem.at[1, k]),
+            pltpu.make_async_copy(w_value.at[:, rows], wkv.at[k, kv_cols:], w_sem.at[2, k]),
+        ]
+
+    def out_copy(j):
+        return pltpu.make_async_copy(
+            w_out.at[:, pl.ds(pl.multiple_of(j * cols, cols), cols)], wo.at[j], wo_sem.at[j]
+        )
+
+    def remote(src, dst, send, recv, peer):
+        return pltpu.make_async_remote_copy(
+            src_ref=src, dst_ref=dst, send_sem=send, recv_sem=recv,
+            device_id={"tp": peer}, device_id_type=pl.DeviceIdType.MESH,
+        )
+
+    def piece_copy(k, src, send, peer):
+        return remote(gathered.at[k, src], gathered.at[k, src], send, g_recv.at[k, src], peer)
+
+    def z_copy(k, d):
+        return piece_copy(k, me, g_zsend.at[k, d - 1], at_z(lax.rem(z + d, NZ)))
+
+    def y_copy(k, d):
+        return piece_copy(k, at_z(lax.rem(z + d, NZ)), g_ysend.at[k, d], y_peer)
+
+    def c_copy(k, d, yy):
+        src = (lax.rem(z + d, NZ) * NY + yy) * NC + core
+        return piece_copy(k, src, g_csend.at[k, d, yy], core_peer)
+
+    barrier = pltpu.get_barrier_semaphore()
+
+    def greet(d, carry):
+        pl.semaphore_signal(
+            barrier, inc=1, device_id={"tp": lax.rem(me + d, N)},
+            device_id_type=pl.DeviceIdType.MESH,
+        )
+        return carry
+
+    lax.fori_loop(1, N, greet, 0)
+    for k in range(KC):
+        for copy in weight_copies(k):
+            copy.start()
+
+    values = residual[...]
+    inv = lax.rsqrt(jnp.mean(values * values, axis=1, keepdims=True) + 1e-05)
+    for k in range(KC):
+        for q in range(SUB):
+            at = k * chunk + q * width
+            pack[k, q * OWN:(q + 1) * OWN, :] = (
+                residual[:, at:at + width] * inv * gain[:, at:at + width]
+            )
+        gathered[k, me] = pack[k].astype(jnp.bfloat16)
+    pl.semaphore_wait(barrier, N - 1)
+
+    def send_own(k, carry):
+        c_copy(k, 0, y).start()
+        y_copy(k, 0).start()
+        for d in (1, 2, 3):
+            z_copy(k, d).start()
+        return carry
+
+    lax.fori_loop(0, KC, send_own, 0)
+
+    q_acc[...] = jnp.zeros_like(q_acc)
+    kv_acc[...] = jnp.zeros_like(kv_acc)
+
+    row_i = lax.broadcasted_iota(jnp.int32, (tokens, tokens), 0)
+    col_i = lax.broadcasted_iota(jnp.int32, (tokens, tokens), 1)
+    row_tok, col_tok = token_of_row(row_i), token_of_row(col_i)
+    seg_plain = jnp.broadcast_to(segments[...], (tokens, tokens))
+    seg_col = jnp.sum(jnp.where(col_i == row_tok, seg_plain, 0), axis=1, keepdims=True)
+    seg_col_plain = jnp.sum(jnp.where(col_i == row_i, seg_plain, 0), axis=1, keepdims=True)
+    seg_row = jnp.sum(jnp.where(row_i == col_tok, seg_col_plain, 0), axis=0, keepdims=True)
+    start_col = jnp.sum(jnp.where(seg_plain < seg_col, 1, 0), axis=1, keepdims=True)
+    start_row = jnp.sum(jnp.where(seg_col_plain < seg_row, 1, 0), axis=0, keepdims=True)
+    allowed = (col_tok <= row_tok) & (seg_col == seg_row)
+    half = HD // 2
+    pos_col = (row_tok[:, :half] - start_col).astype(jnp.float32)
+    pos_row = (col_tok[:half, :] - start_row).astype(jnp.float32)
+    log_base = math.log(rope_base)
+    freq_lane = jnp.exp(col_i[:, :half].astype(jnp.float32) * (-2.0 * log_base / HD))
+    freq_row = jnp.exp(row_i[:half, :].astype(jnp.float32) * (-2.0 * log_base / HD))
+    cos_q, sin_q = jnp.cos(pos_col * freq_lane), jnp.sin(pos_col * freq_lane)
+    cos_k, sin_k = jnp.cos(pos_row * freq_row), jnp.sin(pos_row * freq_row)
+
+    pr = lax.broadcasted_iota(jnp.int32, (N * 16, N * 16), 0)
+    pc = lax.broadcasted_iota(jnp.int32, (N * 16, N * 16), 1)
+    tok = token_of_row(pr % tokens)
+    order = one_hot(pc == (tok // OWN) * 16 + (pr // tokens) * OWN + tok % OWN)
+
+    def gather_step(s, carry):
+        @pl.when(s < KC)
+        def _():
+            for d in (1, 2, 3):
+                piece_copy(s, at_z(lax.rem(z + d, NZ)), g_zsend.at[s, 0], y_peer).wait_recv()
+                y_copy(s, d).start()
+                c_copy(s, d, y).start()
+
+        @pl.when((s >= 1) & (s < KC + 1))
+        def _():
+            k = s - 1
+            for d in range(NZ):
+                src = (lax.rem(z + d, NZ) * NY + (1 - y)) * NC + core
+                piece_copy(k, src, g_zsend.at[k, 0], y_peer).wait_recv()
+                c_copy(k, d, 1 - y).start()
+            for copy in weight_copies(k):
+                copy.wait()
+            for i in range(RC // KC):
+                out_copy(k * (RC // KC) + i).start()
+
+        @pl.when(s >= 2)
+        def _():
+            k = s - 2
+            for d in range(N // 2):
+                src = d * NC + (1 - core)
+                piece_copy(k, src, g_zsend.at[k, 0], y_peer).wait_recv()
+            rows = dot(order, gathered[k].reshape(N * 16, width)).astype(jnp.bfloat16)
+            for q in range(SUB):
+                lhs = rows[q * tokens:(q + 1) * tokens]
+                at = pl.ds(pl.multiple_of(k * chunk + q * width, width), width)
+                q_acc[...] += dot(lhs, wq[at, :])
+                kv_acc[...] += dot_t(wkv[k, :, q * width:(q + 1) * width], lhs)
+
+        return carry
+
+    lax.fori_loop(0, KC + 2, gather_step, 0)
+
+    sr = lax.broadcasted_iota(jnp.int32, (HD, HD), 0)
+    sc = lax.broadcasted_iota(jnp.int32, (HD, HD), 1)
+    source = ((sr // 8) % 2) * kv_cols + (sr % 8) * KVH + sr // 16
+    turned = dot(one_hot(sc == source), kv_acc[...].astype(jnp.bfloat16))
+    turned = jnp.concatenate([turned, turned], axis=1).astype(jnp.bfloat16)
+    kv_out[...] = turned.reshape(KVH, 16, HD)
+
+    def kv_copy(d):
+        peer = lax.rem(me + d, N)
+        return remote(kv_out.at[peer // 2], kv_in.at[me], kv_send.at[d], kv_recv.at[me], peer)
+
+    def kv_start(d, carry):
+        kv_copy(d).start()
+        return carry
+
+    lax.fori_loop(1, N, kv_start, 0)
+    kv_in[me] = kv_out[me // 2]
+
+    scale = 1.0 / math.sqrt(HD)
+    queries = []
+    for h in range(heads):
+        lin = q_acc[:, h * HD:(h + 1) * HD].astype(jnp.bfloat16).astype(jnp.float32)
+        a, b = lin[:, :half], lin[:, half:]
+        queries.append(
+            jnp.concatenate([a * cos_q - b * sin_q, b * cos_q + a * sin_q], axis=1)
+        )
+
+    def kv_wait(d, carry):
+        src = lax.rem(me + d, N)
+        remote(kv_out.at[0], kv_in.at[src], kv_send.at[d], kv_recv.at[src], src).wait_recv()
+        return carry
+
+    lax.fori_loop(1, N, kv_wait, 0)
+    kv = kv_in[...].astype(jnp.float32)
+    keys = kv[:, :8, :tokens].reshape(HD, tokens)
+    vals = kv[:, 8:, :tokens].reshape(HD, tokens).astype(jnp.bfloat16)
+    a, b = keys[:half], keys[half:]
+    keys = jnp.concatenate([a * cos_k - b * sin_k, b * cos_k + a * sin_k], axis=0)
+    keys = keys.astype(jnp.bfloat16)
+    for h in range(heads):
+        scores = dot(queries[h].astype(jnp.bfloat16), keys) * scale
+        scores = jnp.where(allowed, scores, -1e30)
+        weights = jnp.exp(scores - jnp.max(scores, axis=1, keepdims=True))
+        probs = (weights / jnp.sum(weights, axis=1, keepdims=True)).astype(jnp.bfloat16)
+        attended[:, h * HD:(h + 1) * HD] = dot_t(probs, vals).astype(jnp.bfloat16)
+
+    zr = lax.broadcasted_iota(jnp.int32, (64, 64), 0)
+    zc = lax.broadcasted_iota(jnp.int32, (64, 64), 1)
+    by_z = one_hot(zc == ((zr // OWN) % SUB) * 16 + (zr // 16) * OWN + zr % OWN)
+
+    def core_copy(j):
+        return remote(core_out.at[j], core_in.at[j], c_send.at[j], c_recv.at[j], core_peer)
+
+    def row_copy(j):
+        return remote(y_out.at[j], y_in.at[j], y_send.at[j], y_recv.at[j], y_peer)
+
+    def line_copy(j, d):
+        zz = lax.rem(z + d, NZ)
+        return remote(
+            z_out.at[j, zz], z_in.at[j, z], z_send.at[j, d - 1], z_recv.at[j, z], at_z(zz)
+        )
+
+    def sum_step(s, carry):
+        @pl.when(s < RC)
+        def _():
+            out_copy(s).wait()
+            part = dot(attended[...], wo[s]).reshape(2, 32, cols)
+            low, high = part[0], part[1]
+            core_out[s] = jnp.where(core == 0, high, low).astype(jnp.bfloat16)
+            core_copy(s).start()
+            core_own[s] = jnp.where(core == 0, low, high)
+
+        @pl.when((s >= 1) & (s < RC + 1))
+        def _():
+            j = s - 1
+            core_copy(j).wait_recv()
+            both = core_own[j] + core_in[j].astype(jnp.float32)
+            low, high = both[:16], both[16:]
+            y_out[j] = jnp.where(y == 0, high, low).astype(jnp.bfloat16)
+            row_copy(j).start()
+            y_own[j] = jnp.where(y == 0, low, high)
+
+        @pl.when(s >= 2)
+        def _():
+            j = s - 2
+            row_copy(j).wait_recv()
+            both = y_own[j] + y_in[j].astype(jnp.float32)
+            stacked = jnp.concatenate(
+                [both[:, q * quarter:(q + 1) * quarter] for q in range(SUB)], axis=0
+            )
+            sorted_rows = dot(by_z, stacked.astype(jnp.bfloat16)).astype(jnp.bfloat16)
+            z_out[j] = sorted_rows.reshape(NZ, 16, quarter)
+            for d in (1, 2, 3):
+                line_copy(j, d).start()
+
+        return carry
+
+    lax.fori_loop(0, RC + 2, sum_step, 0)
+
+    for j in range(RC):
+        summed = z_out[j, z].astype(jnp.float32)
+        for d in (1, 2, 3):
+            zz = lax.rem(z + d, NZ)
+            remote(
+                z_out.at[j, zz], z_in.at[j, zz], z_send.at[j, 0], z_recv.at[j, zz], at_z(zz)
+            ).wait_recv()
+            summed = summed + z_in[j, zz].astype(jnp.float32)
+        total[j] = summed
+        for q in range(SUB):
+            at = j * cols + q * quarter
+            out[:, at:at + quarter] = total[j, q * OWN:(q + 1) * OWN, :]
+
+    def sent_gather(k, carry):
+        for d in range(NZ):
+            if d > 0:
+                z_copy(k, d).wait_send()
+            y_copy(k, d).wait_send()
+            c_copy(k, d, 0).wait_send()
+            c_copy(k, d, 1).wait_send()
+        return carry
+
+    def sent_kv(d, carry):
+        kv_copy(d).wait_send()
+        return carry
+
+    def sent_sum(j, carry):
+        core_copy(j).wait_send()
+        row_copy(j).wait_send()
+        for d in (1, 2, 3):
+            line_copy(j, d).wait_send()
+        return carry
+
+    lax.fori_loop(0, KC, sent_gather, 0)
+    lax.fori_loop(1, N, sent_kv, 0)
+    lax.fori_loop(0, RC, sent_sum, 0)
+
+
+def per_device_kernel(residual, norm_gain, segment_ids, w_query, w_key, w_value, w_out):
+    depth, head_cols = w_query.shape
+    kv_cols = w_key.shape[1]
+    tokens = segment_ids.shape[0]
+    width = depth // KC // SUB
+    cols = depth // RC
+    quarter = cols // SUB
+    f32, bf16 = jnp.float32, jnp.bfloat16
+    vmem = pl.BlockSpec(memory_space=pltpu.VMEM)
+    hbm = pl.BlockSpec(memory_space=pl.ANY)
+    dma = pltpu.SemaphoreType.DMA
+    summed = pl.pallas_call(
+        layer_kernel,
+        out_shape=jax.ShapeDtypeStruct(residual.shape, f32),
+        in_specs=[vmem, vmem, vmem, hbm, hbm, hbm, hbm],
+        out_specs=vmem,
+        scratch_shapes=[
+            pltpu.VMEM((KC, 16, width), f32),
+            pltpu.VMEM((KC, N, 16, width), bf16),
+            pltpu.VMEM((depth, head_cols), bf16),
+            pltpu.VMEM((KC, 2 * kv_cols, depth // KC), bf16),
+            pltpu.VMEM((RC, head_cols, cols), bf16),
+            pltpu.VMEM((tokens, head_cols), f32),
+            pltpu.VMEM((2 * kv_cols, tokens), f32),
+            pltpu.VMEM((KVH, 16, HD), bf16),
+            pltpu.VMEM((N, 16, HD), bf16),
+            pltpu.VMEM((tokens, head_cols), bf16),
+            pltpu.VMEM((RC, 32, cols), f32),
+            pltpu.VMEM((RC, 32, cols), bf16),
+            pltpu.VMEM((RC, 32, cols), bf16),
+            pltpu.VMEM((RC, 16, cols), f32),
+            pltpu.VMEM((RC, 16, cols), bf16),
+            pltpu.VMEM((RC, 16, cols), bf16),
+            pltpu.VMEM((RC, NZ, 16, quarter), bf16),
+            pltpu.VMEM((RC, NZ, 16, quarter), bf16),
+            pltpu.VMEM((RC, 16, quarter), f32),
+            dma((3, KC)),
+            dma((RC,)),
+            dma((KC, N)),
+            dma((KC, NZ - 1)),
+            dma((KC, NZ)),
+            dma((KC, NZ, NY)),
+            dma((N,)),
+            dma((N,)),
+            dma((RC,)),
+            dma((RC,)),
+            dma((RC,)),
+            dma((RC,)),
+            dma((RC, NZ - 1)),
+            dma((RC, NZ)),
+        ],
+        compiler_params=pltpu.CompilerParams(
+            collective_id=0, has_side_effects=True, vmem_limit_bytes=60 * 1024 * 1024
+        ),
+        name="sublayer",
+    )(
+        residual, norm_gain.reshape(1, -1), segment_ids.reshape(1, -1),
+        w_query, w_key.T, w_value.T, w_out,
+    )
+    return residual + summed
 
 
 def quantize(values):
@@ -73,7 +453,7 @@
     return outputs.astype(jnp.bfloat16).reshape(token_count, -1)
 
 
-def per_device(residual, norm_gain, segment_ids, w_query, w_key, w_value, w_out):
+def per_device_general(residual, norm_gain, segment_ids, w_query, w_key, w_value, w_out):
     own_rows = residual.shape[0]
     mean_square = jnp.mean(residual * residual, axis=1, keepdims=True)
     normed = residual * lax.rsqrt(mean_square + 1e-05) * norm_gain[None, :]
@@ -128,6 +508,7 @@
         P("tp", None),
     )
     out_specs = P(("groups", "tp"), None)
+    body = per_device_kernel if mesh.shape["tp"] == N else per_device_general
     return jax.shard_map(
-        per_device, mesh=mesh, in_specs=in_specs, out_specs=out_specs, check_vma=False
-    )
+        body, mesh=mesh, in_specs=in_specs, out_specs=out_specs, check_vma=False
+    )

time: 214 us -> 60.9 us (0.28)
  the two profiles are of different devices: /device:TPU:15 before, /device:TPU:0 now
where the time goes in v1:
time: 60.9 us; the launch traced here: 60.8 us
  Pallas kernels  59 us (97%)
  other arithmetic  1.72 us (3%)
    pallas_call x1, Pallas kernels, per_device_kernel(): pl.pallas_call(layer_kernel, out_shape=jax.ShapeDtypeStruct(residual.shap...  59 us
    add x1, other arithmetic, per_device_kernel(): return residual + summed  1.72 us

profile of v1, /device:TPU:0, one launch (start us, length us, event | category | flops | bytes accessed | tf_op | source)
XLA Modules:
  0.0 60.8 jit_solution(9281367217916385330)
XLA Ops:
  0.0 0.0 copy-start
  0.0 59.0 %sublayer.1 = f32[4,16384]{1,0:T(4,128)} custom-call(f32[4,16384]{1,0:T(4,128)} %residual.1, f32[1,16384]{1,0:T(1,128)} %bitcast.6, s32[1,64]{1,0:T(1,128)} %bitcast.7, bf16[16384,512]{1,0:T(8,128)(2,1)} %w_query.1, bf16[64,16384]{1,0:T(8,128)(2,1)} %bitcast.4, bf16[64,16384]{1,0:T(8,128)(2,1)} %bitcast.5, bf16[512,16384]{1,0:T(8,128)(2,1)} %w_out.1), custom_call_target="tpu_custom_call" | custom-call | tf_op jit(solution)/shard_map/sublayer/pallas_call | solution.py:347
  59.0 0.0 copy-done
  59.1 1.7 %add.3 = f32[4,16384]{1,0:T(4,128)} add(f32[4,16384]{1,0:T(4,128)S(1)} %copy-done, f32[4,16384]{1,0:T(4,128)} %sublayer.1) | non-fusion elementwise | flops 65536 | bytes 786432 | tf_op jit(solution)/shard_map/add | solution.py:395
Async XLA Ops:
  0.0 59.0 %copy-start = (f32[4,16384]{1,0:T(4,128)S(1)}, f32[4,16384]{1,0:T(4,128)}, u32[]{:S(2)}) copy-start(f32[4,16384]{1,0:T(4,128)} %residual.1) | copy-start | bytes 786436

commit v2 on v1

--- a/solution.py
+++ b/solution.py
@@ -23,6 +23,7 @@
 SUB = 16 // OWN
 KC = 4
 RC = 8
+CORE_LAG, Y_LAG = 2, 4
 
 
 def one_hot(condition):
@@ -268,9 +269,9 @@
             core_copy(s).start()
             core_own[s] = jnp.where(core == 0, low, high)
 
-        @pl.when((s >= 1) & (s < RC + 1))
+        @pl.when((s >= CORE_LAG) & (s < RC + CORE_LAG))
         def _():
-            j = s - 1
+            j = s - CORE_LAG
             core_copy(j).wait_recv()
             both = core_own[j] + core_in[j].astype(jnp.float32)
             low, high = both[:16], both[16:]
@@ -278,9 +279,9 @@
             row_copy(j).start()
             y_own[j] = jnp.where(y == 0, low, high)
 
-        @pl.when(s >= 2)
+        @pl.when(s >= Y_LAG)
         def _():
-            j = s - 2
+            j = s - Y_LAG
             row_copy(j).wait_recv()
             both = y_own[j] + y_in[j].astype(jnp.float32)
             stacked = jnp.concatenate(
@@ -293,7 +294,7 @@
 
         return carry
 
-    lax.fori_loop(0, RC + 2, sum_step, 0)
+    lax.fori_loop(0, RC + Y_LAG, sum_step, 0)
 
     for j in range(RC):
         summed = z_out[j, z].astype(jnp.float32)

time: 60.9 us -> 57.5 us (0.944)
  Pallas kernels: 59 us -> 55.6 us
    pallas_call x1, Pallas kernels: 59 us -> 55.6 us  [per_device_kernel(): pl.pallas_call(layer_kernel, out_shape=jax.ShapeDtypeStruct(residual.shap...]
where the time goes in v2:
time: 57.5 us; the launch traced here: 57.4 us
  Pallas kernels  55.6 us (97%)
  other arithmetic  1.72 us (3%)
    pallas_call x1, Pallas kernels, per_device_kernel(): pl.pallas_call(layer_kernel, out_shape=jax.ShapeDtypeStruct(residual.shap...  55.6 us
    add x1, other arithmetic, per_device_kernel(): return residual + summed  1.72 us

profile of v2, /device:TPU:0, one launch (start us, length us, event | category | flops | bytes accessed | tf_op | source)
XLA Modules:
  0.0 57.4 jit_solution(15085260795135667266)
XLA Ops:
  0.0 0.0 copy-start
  0.0 55.6 %sublayer.1 = f32[4,16384]{1,0:T(4,128)} custom-call(f32[4,16384]{1,0:T(4,128)} %residual.1, f32[1,16384]{1,0:T(1,128)} %bitcast.6, s32[1,64]{1,0:T(1,128)} %bitcast.7, bf16[16384,512]{1,0:T(8,128)(2,1)} %w_query.1, bf16[64,16384]{1,0:T(8,128)(2,1)} %bitcast.4, bf16[64,16384]{1,0:T(8,128)(2,1)} %bitcast.5, bf16[512,16384]{1,0:T(8,128)(2,1)} %w_out.1), custom_call_target="tpu_custom_call" | custom-call | tf_op jit(solution)/shard_map/sublayer/pallas_call | solution.py:348
  55.7 0.0 copy-done
  55.7 1.7 %add.3 = f32[4,16384]{1,0:T(4,128)} add(f32[4,16384]{1,0:T(4,128)S(1)} %copy-done, f32[4,16384]{1,0:T(4,128)} %sublayer.1) | non-fusion elementwise | flops 65536 | bytes 786432 | tf_op jit(solution)/shard_map/add | solution.py:396
Async XLA Ops:
  0.0 55.7 %copy-start = (f32[4,16384]{1,0:T(4,128)S(1)}, f32[4,16384]{1,0:T(4,128)}, u32[]{:S(2)}) copy-start(f32[4,16384]{1,0:T(4,128)} %residual.1) | copy-start | bytes 786436

commit v3 on v2

--- a/solution.py
+++ b/solution.py
@@ -23,7 +23,7 @@
 SUB = 16 // OWN
 KC = 4
 RC = 8
-CORE_LAG, Y_LAG = 2, 4
+CORE_LAG, Y_LAG, Z_LAG = 2, 4, 7
 
 
 def one_hot(condition):
@@ -92,6 +92,18 @@
     def z_copy(k, d):
         return piece_copy(k, me, g_zsend.at[k, d - 1], at_z(lax.rem(z + d, NZ)))
 
+    def near_line(d):
+        return jnp.logical_not(
+            ((z == 0) & (d == NZ - 1)) | ((z == NZ - 1) & (d == 1))
+        )
+
+    inner = (z == 1) | (z == 2)
+    far = jnp.where(z == 1, NZ - 1, 0)
+    beyond = jnp.where(z == 1, 0, NZ - 1)
+
+    def relay_copy(k):
+        return piece_copy(k, at_z(far), g_zsend.at[k, NZ - 1], at_z(beyond))
+
     def y_copy(k, d):
         return piece_copy(k, at_z(lax.rem(z + d, NZ)), g_ysend.at[k, d], y_peer)
 
@@ -101,14 +113,11 @@
 
     barrier = pltpu.get_barrier_semaphore()
 
-    def greet(d, carry):
+    line = [at_z(lax.rem(z + d, NZ)) for d in range(1, NZ)]
+    for peer in [y_peer, core_peer] + line:
         pl.semaphore_signal(
-            barrier, inc=1, device_id={"tp": lax.rem(me + d, N)},
-            device_id_type=pl.DeviceIdType.MESH,
+            barrier, inc=1, device_id={"tp": peer}, device_id_type=pl.DeviceIdType.MESH
         )
-        return carry
-
-    lax.fori_loop(1, N, greet, 0)
     for k in range(KC):
         for copy in weight_copies(k):
             copy.start()
@@ -122,13 +131,13 @@
                 residual[:, at:at + width] * inv * gain[:, at:at + width]
             )
         gathered[k, me] = pack[k].astype(jnp.bfloat16)
-    pl.semaphore_wait(barrier, N - 1)
+    pl.semaphore_wait(barrier, NZ + 1)
 
     def send_own(k, carry):
         c_copy(k, 0, y).start()
         y_copy(k, 0).start()
         for d in (1, 2, 3):
-            z_copy(k, d).start()
+            pl.when(near_line(d))(lambda: z_copy(k, d).start())
         return carry
 
     lax.fori_loop(0, KC, send_own, 0)
@@ -163,8 +172,16 @@
     def gather_step(s, carry):
         @pl.when(s < KC)
         def _():
-            for d in (1, 2, 3):
-                piece_copy(s, at_z(lax.rem(z + d, NZ)), g_zsend.at[s, 0], y_peer).wait_recv()
+            order_z = (
+                jnp.where(z == 0, 1, z - 1),
+                jnp.where(z == 3, 1, jnp.where(z == 2, 3, 2)),
+                jnp.where(z < 2, 3, 0),
+            )
+            for i, zz in enumerate(order_z):
+                d = lax.rem(zz - z + NZ, NZ)
+                piece_copy(s, at_z(zz), g_zsend.at[s, 0], y_peer).wait_recv()
+                if i == 2:
+                    pl.when(inner)(lambda: relay_copy(s).start())
                 y_copy(s, d).start()
                 c_copy(s, d, y).start()
 
@@ -183,19 +200,32 @@
         @pl.when(s >= 2)
         def _():
             k = s - 2
-            for d in range(N // 2):
-                src = d * NC + (1 - core)
-                piece_copy(k, src, g_zsend.at[k, 0], y_peer).wait_recv()
-            rows = dot(order, gathered[k].reshape(N * 16, width)).astype(jnp.bfloat16)
-            for q in range(SUB):
-                lhs = rows[q * tokens:(q + 1) * tokens]
-                at = pl.ds(pl.multiple_of(k * chunk + q * width, width), width)
-                q_acc[...] += dot(lhs, wq[at, :])
-                kv_acc[...] += dot_t(wkv[k, :, q * width:(q + 1) * width], lhs)
-
-        return carry
-
-    lax.fori_loop(0, KC + 2, gather_step, 0)
+            rows = sorted_rows(k)
+            add_keys(k, rows)
+            add_queries(k, rows)
+
+        return carry
+
+    def sorted_rows(k):
+        for d in range(N // 2):
+            src = d * NC + (1 - core)
+            piece_copy(k, src, g_zsend.at[k, 0], y_peer).wait_recv()
+        return dot(order, gathered[k].reshape(N * 16, width)).astype(jnp.bfloat16)
+
+    def add_keys(k, rows):
+        for q in range(SUB):
+            lhs = rows[q * tokens:(q + 1) * tokens]
+            kv_acc[...] += dot_t(wkv[k, :, q * width:(q + 1) * width], lhs)
+
+    def add_queries(k, rows):
+        for q in range(SUB):
+            lhs = rows[q * tokens:(q + 1) * tokens]
+            at = pl.ds(pl.multiple_of(k * chunk + q * width, width), width)
+            q_acc[...] += dot(lhs, wq[at, :])
+
+    lax.fori_loop(0, KC + 1, gather_step, 0)
+    last_rows = sorted_rows(KC - 1)
+    add_keys(KC - 1, last_rows)
 
     sr = lax.broadcasted_iota(jnp.int32, (HD, HD), 0)
     sc = lax.broadcasted_iota(jnp.int32, (HD, HD), 1)
@@ -214,6 +244,7 @@
 
     lax.fori_loop(1, N, kv_start, 0)
     kv_in[me] = kv_out[me // 2]
+    add_queries(KC - 1, last_rows)
 
     scale = 1.0 / math.sqrt(HD)
     queries = []
@@ -236,12 +267,14 @@
     a, b = keys[:half], keys[half:]
     keys = jnp.concatenate([a * cos_k - b * sin_k, b * cos_k + a * sin_k], axis=0)
     keys = keys.astype(jnp.bfloat16)
+    stacked = jnp.concatenate(queries, axis=0).astype(jnp.bfloat16)
+    scores = dot(stacked, keys) * scale
+    scores = jnp.where(jnp.concatenate([allowed] * heads, axis=0), scores, -1e30)
+    weights = jnp.exp(scores - jnp.max(scores, axis=1, keepdims=True))
+    probs = (weights / jnp.sum(weights, axis=1, keepdims=True)).astype(jnp.bfloat16)
+    mixed = dot_t(probs, vals).astype(jnp.bfloat16)
     for h in range(heads):
-        scores = dot(queries[h].astype(jnp.bfloat16), keys) * scale
-        scores = jnp.where(allowed, scores, -1e30)
-        weights = jnp.exp(scores - jnp.max(scores, axis=1, keepdims=True))
-        probs = (weights / jnp.sum(weights, axis=1, keepdims=True)).astype(jnp.bfloat16)
-        attended[:, h * HD:(h + 1) * HD] = dot_t(probs, vals).astype(jnp.bfloat16)
+        attended[:, h * HD:(h + 1) * HD] = mixed[h * tokens:(h + 1) * tokens]
 
     zr = lax.broadcasted_iota(jnp.int32, (64, 64), 0)
     zc = lax.broadcasted_iota(jnp.int32, (64, 64), 1)
@@ -279,7 +312,7 @@
             row_copy(j).start()
             y_own[j] = jnp.where(y == 0, low, high)
 
-        @pl.when(s >= Y_LAG)
+        @pl.when((s >= Y_LAG) & (s < RC + Y_LAG))
         def _():
             j = s - Y_LAG
             row_copy(j).wait_recv()
@@ -292,27 +325,30 @@
             for d in (1, 2, 3):
                 line_copy(j, d).start()
 
-        return carry
-
-    lax.fori_loop(0, RC + Y_LAG, sum_step, 0)
-
-    for j in range(RC):
-        summed = z_out[j, z].astype(jnp.float32)
-        for d in (1, 2, 3):
-            zz = lax.rem(z + d, NZ)
-            remote(
-                z_out.at[j, zz], z_in.at[j, zz], z_send.at[j, 0], z_recv.at[j, zz], at_z(zz)
-            ).wait_recv()
-            summed = summed + z_in[j, zz].astype(jnp.float32)
-        total[j] = summed
-        for q in range(SUB):
-            at = j * cols + q * quarter
-            out[:, at:at + quarter] = total[j, q * OWN:(q + 1) * OWN, :]
+        @pl.when(s >= Z_LAG)
+        def _():
+            j = s - Z_LAG
+            summed = z_out[j, z].astype(jnp.float32)
+            for d in (1, 2, 3):
+                zz = lax.rem(z + d, NZ)
+                remote(
+                    z_out.at[j, zz], z_in.at[j, zz], z_send.at[j, 0], z_recv.at[j, zz], at_z(zz)
+                ).wait_recv()
+                summed = summed + z_in[j, zz].astype(jnp.float32)
+            total[j] = summed
+            for q in range(SUB):
+                at = pl.ds(pl.multiple_of(j * cols + q * quarter, quarter), quarter)
+                out[:, at] = total[j, q * OWN:(q + 1) * OWN, :]
+
+        return carry
+
+    lax.fori_loop(0, RC + Z_LAG, sum_step, 0)
 
     def sent_gather(k, carry):
+        pl.when(inner)(lambda: relay_copy(k).wait_send())
         for d in range(NZ):
             if d > 0:
-                z_copy(k, d).wait_send()
+                pl.when(near_line(d))(lambda: z_copy(k, d).wait_send())
             y_copy(k, d).wait_send()
             c_copy(k, d, 0).wait_send()
             c_copy(k, d, 1).wait_send()
@@ -373,7 +409,7 @@
             dma((3, KC)),
             dma((RC,)),
             dma((KC, N)),
-            dma((KC, NZ - 1)),
+            dma((KC, NZ)),
             dma((KC, NZ)),
             dma((KC, NZ, NY)),
             dma((N,)),

time: 57.5 us -> 55.4 us (0.963)
  Pallas kernels: 55.6 us -> 53.5 us
    pallas_call x1, Pallas kernels: 55.6 us -> 53.5 us  [per_device_kernel(): pl.pallas_call(layer_kernel, out_shape=jax.ShapeDtypeStruct(residual.shap...]
where the time goes in v3:
time: 55.4 us; the launch traced here: 55.2 us
  Pallas kernels  53.5 us (97%)
  other arithmetic  1.72 us (3%)
    pallas_call x1, Pallas kernels, per_device_kernel(): pl.pallas_call(layer_kernel, out_shape=jax.ShapeDtypeStruct(residual.shap...  53.5 us
    add x1, other arithmetic, per_device_kernel(): return residual + summed  1.72 us

profile of v3, /device:TPU:0, one launch (start us, length us, event | category | flops | bytes accessed | tf_op | source)
XLA Modules:
  0.0 55.2 jit_solution(3631323514147717938)
XLA Ops:
  0.0 0.0 copy-start
  0.0 53.5 %sublayer.1 = f32[4,16384]{1,0:T(4,128)} custom-call(f32[4,16384]{1,0:T(4,128)} %residual.1, f32[1,16384]{1,0:T(1,128)} %bitcast.6, s32[1,64]{1,0:T(1,128)} %bitcast.7, bf16[16384,512]{1,0:T(8,128)(2,1)} %w_query.1, bf16[64,16384]{1,0:T(8,128)(2,1)} %bitcast.4, bf16[64,16384]{1,0:T(8,128)(2,1)} %bitcast.5, bf16[512,16384]{1,0:T(8,128)(2,1)} %w_out.1), custom_call_target="tpu_custom_call" | custom-call | tf_op jit(solution)/shard_map/sublayer/pallas_call | solution.py:384
  53.5 0.0 copy-done
  53.5 1.7 %add.3 = f32[4,16384]{1,0:T(4,128)} add(f32[4,16384]{1,0:T(4,128)S(1)} %copy-done, f32[4,16384]{1,0:T(4,128)} %sublayer.1) | non-fusion elementwise | flops 65536 | bytes 786432 | tf_op jit(solution)/shard_map/add | solution.py:432
Async XLA Ops:
  0.0 53.5 %copy-start = (f32[4,16384]{1,0:T(4,128)S(1)}, f32[4,16384]{1,0:T(4,128)}, u32[]{:S(2)}) copy-start(f32[4,16384]{1,0:T(4,128)} %residual.1) | copy-start | bytes 786436

commit v4 on v3

--- a/solution.py
+++ b/solution.py
@@ -192,8 +192,6 @@
                 src = (lax.rem(z + d, NZ) * NY + (1 - y)) * NC + core
                 piece_copy(k, src, g_zsend.at[k, 0], y_peer).wait_recv()
                 c_copy(k, d, 1 - y).start()
-            for copy in weight_copies(k):
-                copy.wait()
             for i in range(RC // KC):
                 out_copy(k * (RC // KC) + i).start()
 
@@ -210,6 +208,8 @@
         for d in range(N // 2):
             src = d * NC + (1 - core)
             piece_copy(k, src, g_zsend.at[k, 0], y_peer).wait_recv()
+        for copy in weight_copies(k):
+            copy.wait()
         return dot(order, gathered[k].reshape(N * 16, width)).astype(jnp.bfloat16)
 
     def add_keys(k, rows):

time: 55.4 us -> 55.4 us (level)
  no operation moved by 1% of the time
where the time goes in v4:
time: 55.4 us; the launch traced here: 55.3 us
  Pallas kernels  53.5 us (97%)
  other arithmetic  1.72 us (3%)
    pallas_call x1, Pallas kernels, per_device_kernel(): pl.pallas_call(layer_kernel, out_shape=jax.ShapeDtypeStruct(residual.shap...  53.5 us
    add x1, other arithmetic, per_device_kernel(): return residual + summed  1.72 us

profile of v4, /device:TPU:0, one launch (start us, length us, event | category | flops | bytes accessed | tf_op | source)
XLA Modules:
  0.0 55.3 jit_solution(6543856106311916370)
XLA Ops:
  0.0 0.0 copy-start
  0.0 53.5 %sublayer.1 = f32[4,16384]{1,0:T(4,128)} custom-call(f32[4,16384]{1,0:T(4,128)} %residual.1, f32[1,16384]{1,0:T(1,128)} %bitcast.6, s32[1,64]{1,0:T(1,128)} %bitcast.7, bf16[16384,512]{1,0:T(8,128)(2,1)} %w_query.1, bf16[64,16384]{1,0:T(8,128)(2,1)} %bitcast.4, bf16[64,16384]{1,0:T(8,128)(2,1)} %bitcast.5, bf16[512,16384]{1,0:T(8,128)(2,1)} %w_out.1), custom_call_target="tpu_custom_call" | custom-call | tf_op jit(solution)/shard_map/sublayer/pallas_call | solution.py:384
  53.5 0.0 copy-done
  53.5 1.7 %add.3 = f32[4,16384]{1,0:T(4,128)} add(f32[4,16384]{1,0:T(4,128)S(1)} %copy-done, f32[4,16384]{1,0:T(4,128)} %sublayer.1) | non-fusion elementwise | flops 65536 | bytes 786432 | tf_op jit(solution)/shard_map/add | solution.py:432
Async XLA Ops:
  0.0 53.5 %copy-start = (f32[4,16384]{1,0:T(4,128)S(1)}, f32[4,16384]{1,0:T(4,128)}, u32[]{:S(2)}) copy-start(f32[4,16384]{1,0:T(4,128)} %residual.1) | copy-start | bytes 786436
